TPU v7x, 128 devices: a whole 4x4x4 slice. The times are simulated.
128 devices in a mesh: row: 4 (over x), col: 32 (over y, z, core).
Axes of the slice: x: 4, y: 4, z: 4, core: 2. Of those that a mesh axis runs over, the one named last changes fastest.
Arguments:
- pair_slab: bfloat16 [32, 4096, 128], P('row', 'col'), may hold values from -6 to 6
- pair_bias: bfloat16 [4, 4096, 4096], P(None, 'col', 'row'), may hold values from -5 to 240
- tile_mask: int32 [64, 64], replicated, may hold values from 0 to 1, as said below
- w_proj: bfloat16 [128, 512], replicated, may hold values from -0.5 to 0.5
- w_out: bfloat16 [128, 128], replicated, may hold values from -0.5 to 0.5
- d_out: bfloat16 [32, 4096, 128], P('row', 'col'), may hold values from -6 to 6
Outputs:
- attn_out: bfloat16 [32, 4096, 128], P('row', 'col')
- slab_grads: bfloat16 [32, 4096, 128], P('row', 'col')
- bias_grads: float32 [4096, 4, 4096], P(('row', 'col'))
Inputs may be any that keep to these rules, and one draw needn't show every extreme that they name: tile_mask[a, a] is 1 for every tile a, and tile_mask[a, b] is 0 wherever b > a.
All inputs are finite; a program needn't handle non-finite values.
Results may differ from a plain program's by a relative error of at most 0.019.
Values may be sent and summed in bfloat16 or wider, within the bound.
A program may use at most 192 MiB of HBM per device.

v0:
```python
import jax
import jax.numpy as jnp
from jax import lax
from jax.sharding import PartitionSpec as P

H = 4
DH = 32
TILE = 64
eps_norm = 1e-05
neg_big = -1e30


def normalize(pair_slab):
    entries = pair_slab.astype(jnp.float32)
    centred = entries - jnp.mean(entries, axis=-1, keepdims=True)
    spread = jnp.mean(centred * centred, axis=-1, keepdims=True)
    return centred * lax.rsqrt(spread + eps_norm)


def expand_tiles(tile_block):
    grown = jnp.repeat(jnp.repeat(tile_block, TILE, axis=0), TILE, axis=1)
    return (grown > 0)[None, None]


def pair_scores(query_heads, key_heads, bias_block):
    scores = jnp.einsum(
        "rjhd,rkhd->rhjk", query_heads, key_heads, preferred_element_type=jnp.float32
    )
    return scores + bias_block[None].astype(jnp.float32)


def on_device(pair_slab, pair_bias, tile_mask, w_proj, w_out, d_out):
    row_count, col_count, channels = pair_slab.shape
    head_width = H * DH
    q_scale = DH ** (-0.5)
    own_start = lax.axis_index("col") * col_count
    normed_f, norm_pull = jax.vjp(normalize, pair_slab)
    normed = normed_f.astype(jnp.bfloat16)
    flat_normed = normed.reshape(row_count * col_count, channels)
    w_query = w_proj[:, :head_width]
    w_pair = w_proj[:, head_width : 3 * head_width]
    w_gate = w_proj[:, 3 * head_width :]
    w_pair_back = jnp.transpose(w_pair).astype(jnp.float32)
    queries = (jnp.dot(flat_normed, w_query, preferred_element_type=jnp.float32) * q_scale).astype(
        jnp.bfloat16
    )
    query_heads = queries.reshape(row_count, col_count, H, DH)
    gating = jax.nn.sigmoid(jnp.dot(flat_normed, w_gate, preferred_element_type=jnp.float32))
    gating = gating.reshape(row_count, col_count, head_width)
    bias_rows = lax.all_gather(pair_bias, "row", axis=2, tiled=True)
    gathered_slab = lax.all_gather(normed, "col", axis=1, tiled=True)
    key_values = jnp.dot(
        gathered_slab.reshape(-1, channels), w_pair, preferred_element_type=jnp.float32
    )
    key_values = key_values.astype(jnp.bfloat16).reshape(row_count, -1, 2 * head_width)
    total_cols = key_values.shape[1]
    block_len = min(512, total_cols)
    block_count = total_cols // block_len
    block_ids = jnp.arange(block_count, dtype=jnp.int32)

    def key_slices(block_index):
        key_start = block_index * block_len
        chosen = lax.dynamic_slice_in_dim(key_values, key_start, block_len, 1)
        key_heads = chosen[..., :head_width].reshape(row_count, block_len, H, DH)
        value_heads = chosen[..., head_width:].reshape(row_count, block_len, H, DH)
        bias_block = lax.dynamic_slice_in_dim(bias_rows, key_start, block_len, 2)
        tile_block = lax.dynamic_slice(
            tile_mask,
            (own_start // TILE, key_start // TILE),
            (col_count // TILE, block_len // TILE),
        )
        return (key_heads, value_heads, bias_block, tile_block)

    def stats_step(carried, block_index):
        key_heads, value_heads, bias_block, tile_block = key_slices(block_index)

        def stats_live(running):
            running_max, running_sum = running
            active = expand_tiles(tile_block)
            scores = jnp.where(active, pair_scores(query_heads, key_heads, bias_block), neg_big)
            new_max = jnp.maximum(running_max, jnp.max(scores, axis=-1))
            exp_terms = jnp.where(active, jnp.exp(scores - new_max[..., None]), 0.0)
            return (
                new_max,
                running_sum * jnp.exp(running_max - new_max) + jnp.sum(exp_terms, axis=-1),
            )

        return (
            lax.cond(jnp.any(tile_block > 0), stats_live, lambda unchanged: unchanged, carried),
            None,
        )

    start_max = jnp.full((row_count, H, col_count), neg_big, jnp.float32)
    start_sum = jnp.zeros((row_count, H, col_count), jnp.float32)
    (top_score, exp_total), _ = lax.scan(stats_step, (start_max, start_sum), block_ids)
    log_norm = top_score + jnp.log(exp_total)

    def value_step(carried, block_index):
        key_heads, value_heads, bias_block, tile_block = key_slices(block_index)

        def value_live(value_acc):
            active = expand_tiles(tile_block)
            scores = pair_scores(query_heads, key_heads, bias_block)
            weights = jnp.where(active, jnp.exp(scores - log_norm[..., None]), 0.0).astype(
                jnp.bfloat16
            )
            return value_acc + jnp.einsum(
                "rhjk,rkhd->rjhd", weights, value_heads, preferred_element_type=jnp.float32
            )

        return (
            lax.cond(jnp.any(tile_block > 0), value_live, lambda unchanged: unchanged, carried),
            None,
        )

    value_acc, _ = lax.scan(
        value_step, jnp.zeros((row_count, col_count, H, DH), jnp.float32), block_ids
    )
    attended = value_acc.reshape(row_count, col_count, head_width)
    gated = (gating * attended).astype(jnp.bfloat16)
    attn_out = jnp.dot(gated.reshape(-1, head_width), w_out, preferred_element_type=jnp.float32)
    attn_out = attn_out.astype(jnp.bfloat16).reshape(row_count, col_count, channels)
    d_gated = jnp.dot(
        d_out.reshape(-1, channels), jnp.transpose(w_out), preferred_element_type=jnp.float32
    )
    d_gated = d_gated.reshape(row_count, col_count, head_width)
    d_attended = (d_gated * gating).astype(jnp.bfloat16)
    d_gate_lin = d_gated * attended * gating * (1.0 - gating)
    row_delta = jnp.sum(
        (d_attended.astype(jnp.float32) * attended).reshape(row_count, col_count, H, DH), axis=-1
    )
    row_delta = jnp.transpose(row_delta, (0, 2, 1))
    d_att_heads = d_attended.reshape(row_count, col_count, H, DH)

    def grad_step(carried, block_index):
        key_heads, value_heads, bias_block, tile_block = key_slices(block_index)

        def grad_live(d_query_acc):
            active = expand_tiles(tile_block)
            scores = pair_scores(query_heads, key_heads, bias_block)
            probs = jnp.where(active, jnp.exp(scores - log_norm[..., None]), 0.0)
            weights = probs.astype(jnp.bfloat16)
            d_probs = jnp.einsum(
                "rjhd,rkhd->rhjk", d_att_heads, value_heads, preferred_element_type=jnp.float32
            )
            d_scores = probs * (d_probs - row_delta[..., None])
            d_scores_b = d_scores.astype(jnp.bfloat16)
            d_query_acc = d_query_acc + jnp.einsum(
                "rhjk,rkhd->rjhd", d_scores_b, key_heads, preferred_element_type=jnp.float32
            )
            bias_term = jnp.einsum("rhjk->khj", d_scores)
            d_keys = jnp.einsum(
                "rhjk,rjhd->krhd", d_scores_b, query_heads, preferred_element_type=jnp.float32
            )
            d_values = jnp.einsum(
                "rhjk,rjhd->krhd", weights, d_att_heads, preferred_element_type=jnp.float32
            )
            pair_term = jnp.concatenate(
                [
                    d_keys.reshape(block_len, row_count, head_width),
                    d_values.reshape(block_len, row_count, head_width),
                ],
                axis=-1,
            )
            pair_term = jnp.dot(
                pair_term.reshape(block_len * row_count, 2 * head_width),
                w_pair_back,
                precision=lax.Precision.HIGHEST,
            )
            pair_term = pair_term.reshape(block_len, row_count, channels)
            return (d_query_acc, (bias_term, pair_term))

        def skipped(d_query_acc):
            bias_zero = jnp.zeros((block_len, H, col_count), jnp.float32)
            pair_zero = jnp.zeros((block_len, row_count, channels), jnp.float32)
            return (d_query_acc, (bias_zero, pair_zero))

        return lax.cond(jnp.any(tile_block > 0), grad_live, skipped, carried)

    d_query_acc, block_terms = lax.scan(
        grad_step, jnp.zeros((row_count, col_count, H, DH), jnp.float32), block_ids
    )
    bias_terms = block_terms[0].reshape(total_cols, H, col_count)
    pair_terms = block_terms[1].reshape(total_cols, row_count, channels)
    pair_sum = lax.psum_scatter(
        pair_terms.astype(jnp.bfloat16), "col", scatter_dimension=0, tiled=True
    ).astype(jnp.float32)
    pair_back = jnp.transpose(pair_sum, (1, 0, 2)).reshape(-1, channels)
    d_qg = jnp.concatenate(
        [
            d_query_acc.reshape(row_count * col_count, head_width) * q_scale,
            d_gate_lin.reshape(row_count * col_count, head_width),
        ],
        axis=-1,
    ).astype(jnp.bfloat16)
    w_qg_back = jnp.transpose(jnp.concatenate([w_query, w_gate], axis=1))
    d_normed = jnp.dot(d_qg, w_qg_back, preferred_element_type=jnp.float32) + pair_back
    slab_grads = norm_pull(d_normed.reshape(row_count, col_count, channels))[0]
    partial_sum = lax.psum_scatter(
        bias_terms.astype(jnp.bfloat16), "row", scatter_dimension=0, tiled=True
    ).astype(jnp.float32)
    bias_grads = lax.all_to_all(
        partial_sum.astype(jnp.bfloat16), "col", split_axis=0, concat_axis=2, tiled=True
    ).astype(partial_sum.dtype)
    return (attn_out, slab_grads, bias_grads)


def solution(mesh):
    in_specs = (P("row", "col", None), P(None, "col", "row"), P(), P(), P(), P("row", "col", None))
    out_specs = (P("row", "col", None), P("row", "col", None), P(("row", "col"), None, None))
    return jax.shard_map(
        on_device, mesh=mesh, in_specs=in_specs, out_specs=out_specs, check_vma=False
    )
```

profile of v0, /device:TPU:0, one launch (start us, length us, event | category | flops | bytes accessed | tf_op | source)
XLA Modules:
  0.0 813.9 jit_solution(17003910610374804841)
XLA Ops:
  10.9 2.0 fusion.54
  13.0 2.3 copy.97
  15.4 1.5 copy.101
  21.4 47.3 %all-gather.3.cloned.1.call-done = bf16[8,4096,128]{2,1,0:T(8,128)(2,1)} async-done(((bf16[8,128,128]{2,1,0:T(8,128)(2,1)}), bf16[8,4096,128]{2,1,0:T(8,128)(2,1)}) %all-gather.3.cloned.1.call-update) | async-done | bytes 8388624 | tf_op jit(solution)/shard_map/all_gather | solution.py:51
  68.6 14.5 %convolution_convert_fusion = bf16[32768,256]{1,0:T(8,128)(2,1)} fusion(bf16[32768,128]{1,0:T(8,128)(2,1)} %bitcast.185, bf16[128,512]{1,0:T(8,128)(2,1)S(1)} %copy-done.10), kind=kOutput, calls=%fused_computation.54 | convolution fusion | flops 2155872256 | bytes 25231360 | tf_op jit(solution)/shard_map/dot_general | solution.py:52
  83.2 21.3 %copy.102 = bf16[8,4096,256]{1,2,0:T(8,128)(2,1)} copy(bf16[8,4096,256]{2,1,0:T(8,128)(2,1)} %bitcast.178) | data formatting | bytes 33554432 | tf_op jit(solution)/shard_map/while | solution.py:116
  104.4 14.2 %all-gather.5.cloned.1.call-done = bf16[4,128,4096]{1,2,0:T(8,128)(2,1)} async-done(((bf16[4,128,1024]{1,2,0:T(8,128)(2,1)}), bf16[4,128,4096]{1,2,0:T(8,128)(2,1)}) %all-gather.5.cloned.1.call-update) | async-done | bytes 4194320 | tf_op jit(solution)/shard_map/all_gather | solution.py:50
  118.7 36.1 %while.51 = (s32[]{:T(128)}, f32[8,4,128]{2,1,0:T(4,128)S(1)}, f32[8,4,128]{2,1,0:T(4,128)S(1)}, s32[8]{0:T(128)S(1)}, s32[64,64]{0,1:T(8,128)}, /*index=5*/s32[...) while((s32[]{:T(128)}, f32[8,4,128]{2,1,0:T(4,128)S(1)}, ...), condition=%wide.region_8.9_spmd, body=%wide.region_2.8_spmd.sunk | while | flops 151265344 | bytes 24269540 | solution.py:95
  119.9 1.5 compare_reduce_fusion.6
  122.1 8.4 %conditional.6 = ((f32[8,4,128]{2,1,0:T(4,128)S(1)}, f32[8,4,128]{2,1,0:T(4,128)S(1)})) conditional(s32[]{:T(128)} %convert_element_type.205, (f32[8,4,128]{2,1,0:T(4,128)S(1)}, f32[8,4,128]{2,1,0:T(4,128)S(1)}) %tuple.175, (s32[2,8]{0,1:T(8,128)S(1)}, s32[]{:T(128)}, pred[]{:T(512)}, bf16[8,4096,256]{1,2,0:T(8,128)(2,1)}, ...), branch_computations={%region_4.4_spmd, %region_5.7_spmd} | conditional | flops 151265296 | bytes 24268952 | solution.py:89
  123.5 1.8 constant_dynamic-slice_fusion
  125.3 3.0 fusion.1
  128.3 2.1 select_reduce_fusion
  131.8 1.5 compare_reduce_fusion.6
  135.2 1.5 compare_reduce_fusion.6
  138.7 1.5 compare_reduce_fusion.6
  142.2 1.5 compare_reduce_fusion.6
  145.6 1.5 compare_reduce_fusion.6
  149.1 1.5 compare_reduce_fusion.6
  152.6 1.5 compare_reduce_fusion.6
  156.2 37.0 %while.52 = (s32[]{:T(128)}, f32[8,128,4,32]{1,3,2,0:T(8,128)}, s32[8]{0:T(128)S(1)}, s32[64,64]{0,1:T(8,128)}, s32[]{:T(128)}, /*index=5*/bf16[8,4096,256]{1,2,...) while((s32[]{:T(128)}, f32[8,128,4,32]{1,3,2,0:T(8,128)}, ...), condition=%wide.region_13.14_spmd, body=%wide.region_9.13_spmd.sunk | while | flops 277217376 | bytes 10375892 | solution.py:116
  157.5 1.4 compare_reduce_fusion.7
  159.5 10.1 %conditional.7 = (f32[8,128,4,32]{1,3,2,0:T(8,128)}) conditional(s32[]{:T(128)} %convert_element_type.206, f32[8,128,4,32]{1,3,2,0:T(8,128)} %get-tuple-element.1564, (s32[2,8]{0,1:T(8,128)S(1)}, s32[]{:T(128)}, pred[]{:T(512)}, bf16[8,4096,256]{1,2,0:T(8,128)(2,1)}, bf16[8,128,4,32]{1,3,2,0:T(8,128)(2,1)}, ...), branch_computations={%region_11.11_spmd, %region_12.12_spmd} | conditional | flops 277217312 | bytes 10375321 | solution.py:112
  159.5 3.3 constant_dynamic-slice_fusion.2
  164.8 4.8 fusion.14
  170.9 1.4 compare_reduce_fusion.7
  174.3 1.4 compare_reduce_fusion.7
  177.7 1.4 compare_reduce_fusion.7
  181.0 1.4 compare_reduce_fusion.7
  193.2 2.3 bitcast_reduce_fusion
  196.4 97.8 %while.53 = (s32[]{:T(128)}, f32[8,128,4,32]{1,3,2,0:T(8,128)}, bf16[8,512,4,128]{3,1,0,2:T(8,128)(2,1)}, bf16[8,512,8,128]{3,2,1,0:T(8,128)(2,1)}, s32[8]{0:T(1...) while((s32[]{:T(128)}, f32[8,128,4,32]{1,3,2,0:T(8,128)}, ...), condition=%wide.region_20.21_spmd, body=%wide.region_15.20_spmd.sunk | while | flops 2305949696 | bytes 124179344 | solution.py:180
  199.8 34.9 %conditional.8 = (f32[8,128,4,32]{1,3,2,0:T(8,128)}, bf16[1,512,4,128]{3,1,2,0:T(8,128)(2,1)}, bf16[1,512,8,128]{3,1,2,0:T(8,128)(2,1)S(1)}) conditional(s32[]{:T(128)} %convert_element_type.207, f32[8,128,4,32]{1,3,2,0:T(8,128)} %get-tuple-element.1617, (s32[2,8]{0,1:T(8,128)S(1)}, s32[]{:T(128)}, pred[]{:T(512)}, ...), branch_computations={%region_17.17_spmd, %region_18.19_spmd} | conditional | flops 2305949696 | bytes 121032976 | solution.py:178
  199.8 3.3 constant_dynamic-slice_fusion.4
  204.3 5.5 fusion.75
  210.0 6.9 fusion.73
  216.9 2.9 fusion.39
  219.8 1.8 fusion.26
  221.6 1.8 copy.94
  223.4 3.7 fusion.29
  227.2 1.9 copy.93
  229.0 5.6 fusion.33
  234.7 1.9 bitcast_dynamic-update-slice_fusion.2
  236.6 1.7 copy_dynamic-update-slice_fusion.2
  242.7 1.9 bitcast_dynamic-update-slice_fusion.2
  244.6 1.7 copy_dynamic-update-slice_fusion.2
  250.6 1.9 bitcast_dynamic-update-slice_fusion.2
  252.5 1.6 copy_dynamic-update-slice_fusion.2
  258.6 1.9 bitcast_dynamic-update-slice_fusion.2
  260.5 1.7 copy_dynamic-update-slice_fusion.2
  266.6 2.0 bitcast_dynamic-update-slice_fusion.2
  268.6 1.7 copy_dynamic-update-slice_fusion.2
  274.6 1.9 bitcast_dynamic-update-slice_fusion.2
  276.6 1.6 copy_dynamic-update-slice_fusion.2
  282.6 1.9 bitcast_dynamic-update-slice_fusion.2
  284.5 1.7 copy_dynamic-update-slice_fusion.2
  290.5 2.0 bitcast_dynamic-update-slice_fusion.2
  292.5 1.7 copy_dynamic-update-slice_fusion.2
  294.8 412.0 %reduce-scatter.5.cloned.1.call-done = bf16[1024,4,128]{2,0,1:T(8,128)(2,1)} async-done(((bf16[4096,4,128]{2,0,1:T(8,128)(2,1)}), bf16[1024,4,128]{2,0,1:T(8,128)(2,1)}) %reduce-scatter.5.cloned.1.call-update) | async-done | bytes 1048592 | tf_op jit(solution)/shard_map/reduce_scatter | solution.py:199
  706.9 3.0 copy.118
  709.9 7.3 all-to-all-start
  723.2 2.0 convolution_convert_fusion.1
  725.2 8.8 %all-to-all-done = bf16[1024,4,128]{2,1,0:T(4,128)(2,1)S(1)} async-done(((bf16[1024,4,128]{2,1,0:T(4,128)(2,1)}), bf16[1024,4,128]{2,1,0:T(4,128)(2,1)S(1)}, u32[]{:S(2)}, u32[]{:S(2)}) %all-to-all-start) | async-done | bytes 1048608 | tf_op jit(solution)/shard_map/all_to_all | solution.py:202
  735.6 1.7 reshape.247
  737.3 66.2 %reduce-scatter.3.cloned.1.call-done = bf16[128,8,128]{2,1,0:T(8,128)(2,1)} async-done(((bf16[4096,8,128]{2,1,0:T(8,128)(2,1)}), bf16[128,8,128]{2,1,0:T(8,128)(2,1)}) %reduce-scatter.3.cloned.1.call-update) | async-done | bytes 262160 | tf_op jit(solution)/shard_map/reduce_scatter | solution.py:185
  (183 shorter events, 71.7 us)
Async XLA Ops:
  7.2 186.1 %copy-start = (bf16[8,128,128]{2,1,0:T(8,128)(2,1)S(1)}, bf16[8,128,128]{2,1,0:T(8,128)(2,1)}, u32[]{:S(2)}) copy-start(bf16[8,128,128]{2,1,0:T(8,128)(2,1)} %param.23) | copy-start | bytes 786436
  7.2 14.0 %slice-start = ((bf16[128,512]{1,0:T(8,128)(2,1)}), bf16[128,256]{1,0:T(8,128)(2,1)S(1)}, s32[]{:S(2)}) async-start(bf16[128,512]{1,0:T(8,128)(2,1)} %param.21), calls=%async_computation.7 | async-start | bytes 131072
  7.2 61.5 %copy-start.10 = (bf16[128,512]{1,0:T(8,128)(2,1)S(1)}, bf16[128,512]{1,0:T(8,128)(2,1)}, u32[]{:S(2)}) copy-start(bf16[128,512]{1,0:T(8,128)(2,1)} %param.21) | copy-start | bytes 393220
  7.2 61.4 %all-gather.3.cloned.1.call-start = ((), (), s32[]{:S(2)}) async-start(), calls=%async_computation.3 | async-start | bytes 8650752 | tf_op jit(solution)/shard_map/all_gather | solution.py:51
  8.4 1.9 copy-start.13
  9.7 0.6 copy-start.18
  10.3 0.6 copy-start.16
  13.0 105.7 %all-gather.5.cloned.1.call-start = ((), (), s32[]{:S(2)}) async-start(), calls=%async_computation.4 | async-start | bytes 5242880 | tf_op jit(solution)/shard_map/all_gather | solution.py:50
  15.3 691.6 %reduce-scatter.5.cloned.1.call-start = ((), (), s32[]{:S(2)}) async-start(), calls=%async_computation.6 | async-start | bytes 5242880 | tf_op jit(solution)/shard_map/reduce_scatter | solution.py:199
  20.2 63.0 %copy-start.7 = (f32[1024,128]{1,0:T(8,128)}, f32[1024,128]{1,0:T(8,128)S(1)}, u32[]{:S(2)}) copy-start(f32[1024,128]{1,0:T(8,128)S(1)} %fusion.47) | copy-start | bytes 1572868
  199.8 10.2 %copy-start.20 = (f32[8,4,128]{2,1,0:T(4,128)S(1)}, f32[8,4,128]{2,1,0:T(4,128)}, u32[]{:S(2)}) copy-start(f32[8,4,128]{2,1,0:T(4,128)} %get-tuple-element.1016) | copy-start | bytes 49156 | tf_op jit(solution)/shard_map/while/body/eval_jaxpr/cond
  210.0 9.9 %copy-start.3 = (f32[8,4,512,128]{3,2,1,0:T(8,128)S(1)}, f32[8,4,512,128]{3,2,1,0:T(8,128)}, u32[]{:S(2)}) copy-start(f32[8,4,512,128]{3,2,1,0:T(8,128)} %fusion.75) | copy-start | bytes 25165828 | tf_op jit(solution)/shard_map/while/body/eval_jaxpr/cond
  210.0 9.8 %copy-start.12 = (bf16[8,128,4,32]{1,3,2,0:T(8,128)(2,1)S(1)}, bf16[8,128,4,32]{1,3,2,0:T(8,128)(2,1)}, u32[]{:S(2)}) copy-start(bf16[8,128,4,32]{1,3,2,0:T(8,128)(2,1)} %get-tuple-element.1017) | copy-start | bytes 786436 | tf_op jit(solution)/shard_map/while/body/eval_jaxpr/cond
  216.9 4.7 copy-start.2
  294.2 422.9 %copy-start.11 = (bf16[128,512]{1,0:T(8,128)(2,1)S(1)}, bf16[128,512]{1,0:T(8,128)(2,1)}, u32[]{:S(2)}) copy-start(bf16[128,512]{1,0:T(8,128)(2,1)} %param.21) | copy-start | bytes 393220
  294.2 425.4 %copy-start.5 = (f32[8,128,128]{1,2,0:T(8,128)S(1)}, f32[8,128,128]{1,2,0:T(8,128)}, u32[]{:S(2)}) copy-start(f32[8,128,128]{1,2,0:T(8,128)} %copy.106) | copy-start | bytes 1572868
  294.3 425.4 %copy-start.6 = (f32[8,128,128]{1,2,0:T(8,128)S(1)}, f32[8,128,128]{1,2,0:T(8,128)}, u32[]{:S(2)}) copy-start(f32[8,128,128]{1,2,0:T(8,128)} %get-tuple-element.1269) | copy-start | bytes 1572868
  294.3 509.2 %reduce-scatter.3.cloned.1.call-start = ((), (), s32[]{:S(2)}) async-start(), calls=%async_computation.5 | async-start | bytes 8650752 | tf_op jit(solution)/shard_map/reduce_scatter | solution.py:185
  294.3 428.9 %copy-start.8 = (f32[1024,128]{1,0:T(8,128)S(1)}, f32[1024,128]{1,0:T(8,128)}, u32[]{:S(2)}) copy-start(f32[1024,128]{1,0:T(8,128)} %copy-done.7) | copy-start | bytes 1572868
  294.3 428.9 %copy-start.15 = (bf16[128,128]{1,0:T(8,128)(2,1)S(1)}, bf16[128,128]{1,0:T(8,128)(2,1)}, u32[]{:S(2)}) copy-start(bf16[128,128]{1,0:T(8,128)(2,1)} %param.22) | copy-start | bytes 98308
  709.9 24.1 %all-to-all-start = ((bf16[1024,4,128]{2,1,0:T(4,128)(2,1)}), bf16[1024,4,128]{2,1,0:T(4,128)(2,1)S(1)}, u32[]{:S(2)}, u32[]{:S(2)}) async-start(bf16[1024,4,128]{2,1,0:T(4,128)(2,1)} %copy.118), calls=%async_computation.2 | async-start | bytes 2097152 | tf_op jit(solution)/shard_map/all_to_all | solution.py:202
  725.2 79.4 %copy-start.9 = (bf16[16,8,8,128]{3,1,2,0:T(8,128)(2,1)S(1)}, bf16[16,8,8,128]{3,1,2,0:T(8,128)(2,1)}, u32[]{:S(2)}) copy-start(bf16[16,8,8,128]{3,1,2,0:T(8,128)(2,1)} %copy.145) | copy-start | bytes 786436
  725.2 79.8 %copy-start.4 = (bf16[8,128,128]{2,1,0:T(8,128)(2,1)S(1)}, bf16[8,128,128]{2,1,0:T(8,128)(2,1)}, u32[]{:S(2)}) copy-start(bf16[8,128,128]{2,1,0:T(8,128)(2,1)} %param.18) | copy-start | bytes 786436
  725.2 79.8 %copy-start.14 = (f32[8,128]{1,0:T(8,128)S(1)}, f32[8,128]{1,0:T(8,128)}, u32[]{:S(2)}) copy-start(f32[8,128]{1,0:T(8,128)} %copy-done.13) | copy-start | bytes 12292
  734.1 71.3 %copy-start.19 = (f32[8,128]{1,0:T(8,128)S(1)}, f32[8,128]{1,0:T(8,128)}, u32[]{:S(2)}) copy-start(f32[8,128]{1,0:T(8,128)} %copy-done.18) | copy-start | bytes 12292
  734.1 71.3 %copy-start.17 = (f32[8,128]{1,0:T(8,128)S(1)}, f32[8,128]{1,0:T(8,128)}, u32[]{:S(2)}) copy-start(f32[8,128]{1,0:T(8,128)} %copy-done.16) | copy-start | bytes 12292
  734.1 73.3 %copy-start.1 = (bf16[8,128,128]{2,1,0:T(8,128)(2,1)S(1)}, bf16[8,128,128]{2,1,0:T(8,128)(2,1)}, u32[]{:S(2)}) copy-start(bf16[8,128,128]{2,1,0:T(8,128)(2,1)} %param.23) | copy-start | bytes 786436
Sparse Core Ops, SparseCore 0:
  13.1 55.5 all-gather.2
  70.9 47.7 all-gather.4
  294.4 412.4 reduce-scatter.4
  710.9 92.5 reduce-scatter.2
where the time goes:
time: 820 us; the launch traced here: 814 us
  waiting for transfers between devices  549 us (67%)
  local copies, waits for them, and re-layouts  103 us (13%)
  matrix products  55.8 us (7%)
  other arithmetic  51.1 us (6%)
  loops' own time  33.2 us (4%)
  between operations  14.1 us (2%)
    reduce_scatter x1, waiting for transfers between devices, on_device(): lax.psum_scatter(bias_terms.astype(jnp.bfloat16), 'row', scatter_dimensio...  412 us
    reduce_scatter x1, waiting for transfers between devices, on_device(): lax.psum_scatter(pair_terms.astype(jnp.bfloat16), 'col', scatter_dimensio...  66.2 us
    all_gather x1, waiting for transfers between devices, on_device(): gathered_slab = lax.all_gather(normed, 'col', axis=1, tiled=True)  47.3 us
    dynamic_update_slice x16, local copies, waits for them, and re-layouts, on_device(): lax.scan(grad_step, jnp.zeros((row_count, col_count, H, DH), jnp.float32)...  28.8 us
    while x4, local copies, waits for them, and re-layouts, on_device(): lax.scan(value_step, jnp.zeros((row_count, col_count, H, DH), jnp.float32...  24.8 us
  transfers between devices with their start and end apart: 5, of which 5 were waited for; matrix products, arithmetic and copies ran while one was open for 7% of the time, Pallas kernels for 0%

commit v1 on v0

--- a/solution.py
+++ b/solution.py
@@ -30,6 +30,15 @@
 
 
 def on_device(pair_slab, pair_bias, tile_mask, w_proj, w_out, d_out):
+
+    def move_waves_by_axis(x_part):
+        pieces_in = []
+        for _ in range(jax.lax.axis_size("col")):
+            pieces_in.append(x_part)
+        field_out = jnp.stack(pieces_in, axis=0)
+        current_block = jax.lax.all_to_all(field_out, "col", 0, 0)
+        return jnp.concatenate(current_block, 1)
+
     row_count, col_count, channels = pair_slab.shape
     head_width = H * DH
     q_scale = DH ** (-0.5)
@@ -48,7 +57,7 @@
     gating = jax.nn.sigmoid(jnp.dot(flat_normed, w_gate, preferred_element_type=jnp.float32))
     gating = gating.reshape(row_count, col_count, head_width)
     bias_rows = lax.all_gather(pair_bias, "row", axis=2, tiled=True)
-    gathered_slab = lax.all_gather(normed, "col", axis=1, tiled=True)
+    gathered_slab = move_waves_by_axis(normed)
     key_values = jnp.dot(
         gathered_slab.reshape(-1, channels), w_pair, preferred_element_type=jnp.float32
     )

time: 820 us -> 888 us (1.083)
  waiting for transfers between devices: 549 us -> 590 us
  local copies, waits for them, and re-layouts: 103 us -> 118 us
    all_to_all x0 -> x1, waiting for transfers between devices: none -> 109 us  [move_waves_by_axis(): current_block = jax.lax.all_to_all(field_out, 'col', 0, 0)]
    all_gather x1 -> x0, waiting for transfers between devices: 47.3 us -> none  [on_device(): gathered_slab = lax.all_gather(normed, 'col', axis=1, tiled=True)]
    all_gather x1, waiting for transfers between devices: 14.2 us -> 0.01 us  [on_device(): bias_rows = lax.all_gather(pair_bias, 'row', axis=2, tiled=True)]
    all_to_all x0 -> x1, local copies, waits for them, and re-layouts: none -> 10.4 us  [move_waves_by_axis(): current_block = jax.lax.all_to_all(field_out, 'col', 0, 0)]
  transfers between devices with their start and end apart: 5 -> 5, of which waited for: 5 -> 4; matrix products, arithmetic and copies ran while one was open for 7% -> 7% of each run, Pallas kernels for 0% -> 0%
where the time goes in v1:
time: 888 us; the launch traced here: 876 us
  waiting for transfers between devices  590 us (66%)
  local copies, waits for them, and re-layouts  118 us (13%)
  matrix products  53.1 us (6%)
  other arithmetic  50.5 us (6%)
  loops' own time  33.6 us (4%)
  starting transfers between devices  16 us (2%)
  between operations  14.4 us (2%)
    reduce_scatter x1, waiting for transfers between devices, on_device(): lax.psum_scatter(bias_terms.astype(jnp.bfloat16), 'row', scatter_dimensio...  405 us
    all_to_all x1, waiting for transfers between devices, move_waves_by_axis(): current_block = jax.lax.all_to_all(field_out, 'col', 0, 0)  109 us
    reduce_scatter x1, waiting for transfers between devices, on_device(): lax.psum_scatter(pair_terms.astype(jnp.bfloat16), 'col', scatter_dimensio...  66.3 us
    dynamic_update_slice x16, local copies, waits for them, and re-layouts, on_device(): lax.scan(grad_step, jnp.zeros((row_count, col_count, H, DH), jnp.float32)...  29 us
    while x4, local copies, waits for them, and re-layouts, on_device(): lax.scan(value_step, jnp.zeros((row_count, col_count, H, DH), jnp.float32...  24.6 us
  transfers between devices with their start and end apart: 5, of which 4 were waited for; matrix products, arithmetic and copies ran while one was open for 7% of the time, Pallas kernels for 0%

profile of v1, /device:TPU:0, one launch (start us, length us, event | category | flops | bytes accessed | tf_op | source)
XLA Modules:
  0.0 875.5 jit_solution(18197724401220562661)
XLA Ops:
  12.2 5.4 stack.2
  17.6 8.7 all-to-all-start
  31.1 108.8 %all-to-all-done = bf16[32,8,128,128]{3,2,1,0:T(8,128)(2,1)} async-done(((bf16[32,8,128,128]{3,2,1,0:T(8,128)(2,1)}), bf16[32,8,128,128]{3,2,1,0:T(8,128)(2,1)}, u32[]{:S(2)}, u32[]{:S(2)}) %all-to-all-start) | async-done | bytes 8388640 | tf_op jit(solution)/shard_map/all_to_all | solution.py:39
  139.9 10.4 %copy.95 = bf16[32,8,128,128]{3,2,0,1:T(8,128)(2,1)} copy(bf16[32,8,128,128]{3,2,1,0:T(8,128)(2,1)} %all-to-all-done) | data formatting | bytes 16777216 | tf_op jit(solution)/shard_map/all_to_all | solution.py:39
  150.3 13.6 %convolution_convert_fusion = bf16[32768,256]{1,0:T(8,128)(2,1)} fusion(bf16[32768,128]{1,0:T(8,128)(2,1)} %bitcast.182, bf16[128,512]{1,0:T(8,128)(2,1)S(1)} %copy-done.11), kind=kOutput, calls=%fused_computation.54 | convolution fusion | flops 2155872256 | bytes 25231360 | tf_op jit(solution)/shard_map/dot_general | solution.py:61
  163.9 21.8 %copy.103 = bf16[8,4096,256]{1,2,0:T(8,128)(2,1)} copy(bf16[8,4096,256]{2,1,0:T(8,128)(2,1)} %bitcast.180) | data formatting | bytes 33554432 | tf_op jit(solution)/shard_map/while | solution.py:125
  185.8 36.3 %while.51 = (s32[]{:T(128)}, f32[8,4,128]{2,1,0:T(4,128)S(1)}, f32[8,4,128]{2,1,0:T(4,128)S(1)}, s32[8]{0:T(128)S(1)}, s32[64,64]{0,1:T(8,128)}, /*index=5*/s32[...) while((s32[]{:T(128)}, f32[8,4,128]{2,1,0:T(4,128)S(1)}, ...), condition=%wide.region_8.9_spmd, body=%wide.region_2.8_spmd.sunk | while | flops 151265344 | bytes 24269540 | solution.py:104
  187.0 1.5 compare_reduce_fusion.6
  189.2 8.4 conditional.6
  190.6 1.8 constant_dynamic-slice_fusion
  192.5 3.0 fusion.1
  195.4 2.1 select_reduce_fusion
  198.9 1.5 compare_reduce_fusion.6
  202.4 1.5 compare_reduce_fusion.6
  205.9 1.5 compare_reduce_fusion.6
  209.4 1.5 compare_reduce_fusion.6
  212.9 1.5 compare_reduce_fusion.6
  216.3 1.5 compare_reduce_fusion.6
  219.8 1.5 compare_reduce_fusion.6
  223.5 37.1 %while.52 = (s32[]{:T(128)}, f32[8,128,4,32]{1,3,2,0:T(8,128)}, s32[8]{0:T(128)S(1)}, s32[64,64]{0,1:T(8,128)}, s32[]{:T(128)}, /*index=5*/bf16[8,4096,256]{1,2,...) while((s32[]{:T(128)}, f32[8,128,4,32]{1,3,2,0:T(8,128)}, ...), condition=%wide.region_13.14_spmd, body=%wide.region_9.13_spmd.sunk | while | flops 277217376 | bytes 10375892 | solution.py:125
  224.8 1.4 compare_reduce_fusion.7
  226.8 10.1 %conditional.7 = (f32[8,128,4,32]{1,3,2,0:T(8,128)}) conditional(s32[]{:T(128)} %convert_element_type.206, f32[8,128,4,32]{1,3,2,0:T(8,128)} %get-tuple-element.1564, (s32[2,8]{0,1:T(8,128)S(1)}, s32[]{:T(128)}, pred[]{:T(512)}, bf16[8,4096,256]{1,2,0:T(8,128)(2,1)}, bf16[8,128,4,32]{1,3,2,0:T(8,128)(2,1)}, ...), branch_computations={%region_11.11_spmd, %region_12.12_spmd} | conditional | flops 277217312 | bytes 10375321 | solution.py:121
  226.9 3.3 constant_dynamic-slice_fusion.2
  232.2 4.8 fusion.14
  238.2 1.4 compare_reduce_fusion.7
  241.6 1.4 compare_reduce_fusion.7
  245.0 1.4 compare_reduce_fusion.7
  248.4 1.4 compare_reduce_fusion.7
  260.6 2.3 bitcast_reduce_fusion
  263.8 98.3 %while.53 = (s32[]{:T(128)}, f32[8,128,4,32]{1,3,2,0:T(8,128)}, bf16[8,512,4,128]{3,1,0,2:T(8,128)(2,1)}, bf16[8,512,8,128]{3,2,1,0:T(8,128)(2,1)}, s32[8]{0:T(1...) while((s32[]{:T(128)}, f32[8,128,4,32]{1,3,2,0:T(8,128)}, ...), condition=%wide.region_20.21_spmd, body=%wide.region_15.20_spmd.sunk | while | flops 2305949696 | bytes 124179344 | solution.py:189
  267.3 34.9 %conditional.8 = (f32[8,128,4,32]{1,3,2,0:T(8,128)}, bf16[1,512,4,128]{3,1,2,0:T(8,128)(2,1)}, bf16[1,512,8,128]{3,1,2,0:T(8,128)(2,1)S(1)}) conditional(s32[]{:T(128)} %convert_element_type.207, f32[8,128,4,32]{1,3,2,0:T(8,128)} %get-tuple-element.1617, (s32[2,8]{0,1:T(8,128)S(1)}, s32[]{:T(128)}, pred[]{:T(512)}, ...), branch_computations={%region_17.17_spmd, %region_18.19_spmd} | conditional | flops 2305949696 | bytes 121032976 | solution.py:187
  267.3 3.3 constant_dynamic-slice_fusion.4
  271.8 5.5 fusion.75
  277.5 6.9 fusion.73
  284.4 2.9 fusion.39
  287.4 1.8 fusion.26
  289.2 1.8 copy.94
  291.0 3.7 fusion.29
  294.7 1.8 copy.93
  296.6 5.6 fusion.33
  302.2 1.9 bitcast_dynamic-update-slice_fusion.2
  304.2 1.7 copy_dynamic-update-slice_fusion.2
  310.2 1.9 bitcast_dynamic-update-slice_fusion.2
  312.2 1.7 copy_dynamic-update-slice_fusion.2
  318.2 1.9 bitcast_dynamic-update-slice_fusion.2
  320.2 1.7 copy_dynamic-update-slice_fusion.2
  323.1 1.4 compare_reduce_fusion.8
  326.2 2.0 bitcast_dynamic-update-slice_fusion.2
  328.2 1.7 copy_dynamic-update-slice_fusion.2
  334.3 2.0 bitcast_dynamic-update-slice_fusion.2
  336.3 1.7 copy_dynamic-update-slice_fusion.2
  342.3 1.9 bitcast_dynamic-update-slice_fusion.2
  344.3 1.6 copy_dynamic-update-slice_fusion.2
  350.3 2.0 bitcast_dynamic-update-slice_fusion.2
  352.2 1.7 copy_dynamic-update-slice_fusion.2
  358.3 2.0 bitcast_dynamic-update-slice_fusion.2
  360.2 1.7 copy_dynamic-update-slice_fusion.2
  362.9 405.2 %reduce-scatter.5.cloned.1.call-done = bf16[1024,4,128]{2,0,1:T(8,128)(2,1)} async-done(((bf16[4096,4,128]{2,0,1:T(8,128)(2,1)}), bf16[1024,4,128]{2,0,1:T(8,128)(2,1)}) %reduce-scatter.5.cloned.1.call-update) | async-done | bytes 1048592 | tf_op jit(solution)/shard_map/reduce_scatter | solution.py:208
  768.1 3.0 copy.119
  771.1 7.2 all-to-all-start.1
  784.5 2.0 convolution_convert_fusion.1
  786.4 8.7 all-to-all-done.1
  796.8 1.7 reshape.249
  798.6 66.3 %reduce-scatter.3.cloned.1.call-done = bf16[128,8,128]{2,1,0:T(8,128)(2,1)} async-done(((bf16[4096,8,128]{2,1,0:T(8,128)(2,1)}), bf16[128,8,128]{2,1,0:T(8,128)(2,1)}) %reduce-scatter.3.cloned.1.call-update) | async-done | bytes 262160 | tf_op jit(solution)/shard_map/reduce_scatter | solution.py:194
  (188 shorter events, 71.9 us)
Async XLA Ops:
  7.2 253.4 %copy-start = (bf16[8,128,128]{2,1,0:T(8,128)(2,1)S(1)}, bf16[8,128,128]{2,1,0:T(8,128)(2,1)}, u32[]{:S(2)}) copy-start(bf16[8,128,128]{2,1,0:T(8,128)(2,1)} %param.23) | copy-start | bytes 786436
  8.3 1.9 copy-start.14
  9.7 0.6 copy-start.19
  10.3 0.6 copy-start.17
  17.5 8.8 %copy-start.10 = (bf16[4,128,1024]{2,1,0:T(8,128)(2,1)S(1)}, bf16[4,128,1024]{2,1,0:T(8,128)(2,1)}, u32[]{:S(2)}) copy-start(bf16[4,128,1024]{2,1,0:T(8,128)(2,1)} %param.19) | copy-start | bytes 3145732
  17.6 10.2 %copy-start.21 = (s32[64,64]{1,0:T(8,128)S(1)}, s32[64,64]{1,0:T(8,128)}, u32[]{:S(2)}) copy-start(s32[64,64]{1,0:T(8,128)} %param.20) | copy-start | bytes 49156
  17.6 10.9 %copy-start.11 = (bf16[128,512]{1,0:T(8,128)(2,1)S(1)}, bf16[128,512]{1,0:T(8,128)(2,1)}, u32[]{:S(2)}) copy-start(bf16[128,512]{1,0:T(8,128)(2,1)} %param.21) | copy-start | bytes 393220
  17.6 122.4 %all-to-all-start = ((bf16[32,8,128,128]{3,2,1,0:T(8,128)(2,1)}), bf16[32,8,128,128]{3,2,1,0:T(8,128)(2,1)}, u32[]{:S(2)}, u32[]{:S(2)}) async-start(bf16[32,8,128,128]{3,2,1,0:T(8,128)(2,1)} %stack.2), calls=%async_computation | async-start | bytes 16777216 | tf_op jit(solution)/shard_map/all_to_all | solution.py:39
  26.2 4.7 slice-start
  26.3 159.5 %all-gather.2.cloned.1.call-start = ((), (), s32[]{:S(2)}) async-start(), calls=%async_computation.4 | async-start | bytes 5242880 | tf_op jit(solution)/shard_map/all_gather | solution.py:59
  27.6 740.5 %reduce-scatter.5.cloned.1.call-start = ((), (), s32[]{:S(2)}) async-start(), calls=%async_computation.6 | async-start | bytes 5242880 | tf_op jit(solution)/shard_map/reduce_scatter | solution.py:208
  29.9 120.4 %copy-start.7 = (f32[1024,128]{1,0:T(8,128)}, f32[1024,128]{1,0:T(8,128)S(1)}, u32[]{:S(2)}) copy-start(f32[1024,128]{1,0:T(8,128)S(1)} %fusion.47) | copy-start | bytes 1572868
  267.3 10.2 %copy-start.22 = (f32[8,4,128]{2,1,0:T(4,128)S(1)}, f32[8,4,128]{2,1,0:T(4,128)}, u32[]{:S(2)}) copy-start(f32[8,4,128]{2,1,0:T(4,128)} %get-tuple-element.1016) | copy-start | bytes 49156 | tf_op jit(solution)/shard_map/while/body/eval_jaxpr/cond
  277.5 9.9 %copy-start.3 = (f32[8,4,512,128]{3,2,1,0:T(8,128)S(1)}, f32[8,4,512,128]{3,2,1,0:T(8,128)}, u32[]{:S(2)}) copy-start(f32[8,4,512,128]{3,2,1,0:T(8,128)} %fusion.75) | copy-start | bytes 25165828 | tf_op jit(solution)/shard_map/while/body/eval_jaxpr/cond
  277.5 9.9 %copy-start.13 = (bf16[8,128,4,32]{1,3,2,0:T(8,128)(2,1)S(1)}, bf16[8,128,4,32]{1,3,2,0:T(8,128)(2,1)}, u32[]{:S(2)}) copy-start(bf16[8,128,4,32]{1,3,2,0:T(8,128)(2,1)} %get-tuple-element.1017) | copy-start | bytes 786436 | tf_op jit(solution)/shard_map/while/body/eval_jaxpr/cond
  284.4 4.7 copy-start.2
  362.1 416.2 %copy-start.12 = (bf16[128,512]{1,0:T(8,128)(2,1)S(1)}, bf16[128,512]{1,0:T(8,128)(2,1)}, u32[]{:S(2)}) copy-start(bf16[128,512]{1,0:T(8,128)(2,1)} %param.21) | copy-start | bytes 393220
  362.2 418.7 %copy-start.5 = (f32[8,128,128]{1,2,0:T(8,128)S(1)}, f32[8,128,128]{1,2,0:T(8,128)}, u32[]{:S(2)}) copy-start(f32[8,128,128]{1,2,0:T(8,128)} %copy.107) | copy-start | bytes 1572868
  362.2 418.7 %copy-start.6 = (f32[8,128,128]{1,2,0:T(8,128)S(1)}, f32[8,128,128]{1,2,0:T(8,128)}, u32[]{:S(2)}) copy-start(f32[8,128,128]{1,2,0:T(8,128)} %get-tuple-element.1269) | copy-start | bytes 1572868
  362.2 502.7 %reduce-scatter.3.cloned.1.call-start = ((), (), s32[]{:S(2)}) async-start(), calls=%async_computation.5 | async-start | bytes 8650752 | tf_op jit(solution)/shard_map/reduce_scatter | solution.py:194
  362.2 422.2 %copy-start.8 = (f32[1024,128]{1,0:T(8,128)S(1)}, f32[1024,128]{1,0:T(8,128)}, u32[]{:S(2)}) copy-start(f32[1024,128]{1,0:T(8,128)} %copy-done.7) | copy-start | bytes 1572868
  362.3 422.2 %copy-start.16 = (bf16[128,128]{1,0:T(8,128)(2,1)S(1)}, bf16[128,128]{1,0:T(8,128)(2,1)}, u32[]{:S(2)}) copy-start(bf16[128,128]{1,0:T(8,128)(2,1)} %param.22) | copy-start | bytes 98308
  771.1 24.1 %all-to-all-start.1 = ((bf16[1024,4,128]{2,1,0:T(4,128)(2,1)}), bf16[1024,4,128]{2,1,0:T(4,128)(2,1)S(1)}, u32[]{:S(2)}, u32[]{:S(2)}) async-start(bf16[1024,4,128]{2,1,0:T(4,128)(2,1)} %copy.119), calls=%async_computation.3 | async-start | bytes 2097152 | tf_op jit(solution)/shard_map/all_to_all | solution.py:211
  786.4 79.6 %copy-start.9 = (bf16[16,8,8,128]{3,1,2,0:T(8,128)(2,1)S(1)}, bf16[16,8,8,128]{3,1,2,0:T(8,128)(2,1)}, u32[]{:S(2)}) copy-start(bf16[16,8,8,128]{3,1,2,0:T(8,128)(2,1)} %copy.146) | copy-start | bytes 786436
  786.4 79.9 %copy-start.4 = (bf16[8,128,128]{2,1,0:T(8,128)(2,1)S(1)}, bf16[8,128,128]{2,1,0:T(8,128)(2,1)}, u32[]{:S(2)}) copy-start(bf16[8,128,128]{2,1,0:T(8,128)(2,1)} %param.18) | copy-start | bytes 786436
  786.4 79.9 %copy-start.15 = (f32[8,128]{1,0:T(8,128)S(1)}, f32[8,128]{1,0:T(8,128)}, u32[]{:S(2)}) copy-start(f32[8,128]{1,0:T(8,128)} %copy-done.14) | copy-start | bytes 12292
  795.3 71.5 %copy-start.20 = (f32[8,128]{1,0:T(8,128)S(1)}, f32[8,128]{1,0:T(8,128)}, u32[]{:S(2)}) copy-start(f32[8,128]{1,0:T(8,128)} %copy-done.19) | copy-start | bytes 12292
  795.3 71.5 %copy-start.18 = (f32[8,128]{1,0:T(8,128)S(1)}, f32[8,128]{1,0:T(8,128)}, u32[]{:S(2)}) copy-start(f32[8,128]{1,0:T(8,128)} %copy-done.17) | copy-start | bytes 12292
  795.3 73.4 %copy-start.1 = (bf16[8,128,128]{2,1,0:T(8,128)(2,1)S(1)}, bf16[8,128,128]{2,1,0:T(8,128)(2,1)}, u32[]{:S(2)}) copy-start(bf16[8,128,128]{2,1,0:T(8,128)(2,1)} %param.23) | copy-start | bytes 786436
Sparse Core Ops, SparseCore 0:
  29.3 49.5 all-gather.1
  362.3 405.7 reduce-scatter.4
  772.3 92.5 reduce-scatter.2
